TPU v7x, 256 devices: a whole 4x4x8 slice. The times are simulated.
256 devices in a mesh: ens: 8 (over z_lo, y), space: 32 (over x, z_hi, core).
Axes of the slice: x: 4, y: 4, z: 8 (z_hi: 4, z_lo: 2; z = z_hi * 2 + z_lo), core: 2. Of those that a mesh axis runs over, the one named last changes fastest.
Arguments:
- hidden: bfloat16 [8, 1024, 32768], P('ens', None, 'space'), may hold values from -6 to 6
- target: float32 [100, 32768], P(None, 'space'), may hold values from -6 to 6
- area_index: int32 [32768], P('space'), may hold values from 0 to 720
- area_table: float32 [721], replicated, may hold values from 0.1 to 3
- var_weight: float32 [100], replicated, may hold values from 0.25 to 2
- w_first: bfloat16 [1024, 1024], replicated, may hold values from -0.1875 to 0.1875
- b_first: float32 [1024], replicated, may hold values from -3 to 3
- w_second: bfloat16 [1024, 100], replicated, may hold values from -0.1875 to 0.1875
- b_second: float32 [100], replicated, may hold values from -3 to 3
Outputs:
- loss: float32 [], replicated
- grad_hidden: bfloat16 [8, 1024, 32768], P('ens', None, 'space')
- grad_w_first: float32 [1024, 1024], P('space')
- grad_b_first: float32 [1024], P('space')
- grad_w_second: float32 [1024, 100], P('space')
- grad_b_second: float32 [100], replicated
All inputs are finite; a program needn't handle non-finite values.
Results may differ from a plain program's by a relative error of at most 0.011.
Values sent between devices are 32-bit elements; how exact they have to be, the bound alone decides.
No kernel may reach another device: no remote copies, remote signals or barrier semaphores. Data moves between devices by JAX's collectives and lax.ppermute only.
A program may use at most 64 MiB of HBM per device.

v0:
```python
import math
import jax
import jax.numpy as jnp
from jax import lax
from jax.sharding import PartitionSpec as P

smoothing = 0.0025
loss_scale = 64.0


def pair_terms(fields, others):
    differ = fields - others
    radius = jnp.sqrt(differ * differ + smoothing)
    return (jnp.sum(radius, axis=0), jnp.sum(differ / radius, axis=0))


def on_device(
    hidden, target, area_index, area_table, var_weight, w_first, b_first, w_second, b_second
):
    members = lax.axis_size("ens")
    columns = hidden.shape[2]
    features = hidden[0]
    pre = (
        jnp.einsum("io,ip->op", w_first, features, preferred_element_type=jnp.float32)
        + b_first[:, None]
    )
    hidden_act = jax.nn.gelu(pre).astype(jnp.bfloat16)
    mine = (
        jnp.einsum("ov,op->vp", w_second, hidden_act, preferred_element_type=jnp.float32)
        + b_second[:, None]
    )
    table_rows = area_table.shape[0]
    onehot = (area_index[:, None] == jnp.arange(table_rows, dtype=jnp.int32)[None, :]).astype(
        jnp.float32
    )
    area = jnp.dot(onehot, area_table, precision=lax.Precision.HIGHEST)
    coef = var_weight[:, None] * area[None, :]
    spread_add, pull_add = pair_terms(
        mine[None], lax.all_gather(mine[None], "ens", axis=0, tiled=True)
    )
    miss = mine - target
    skill = jnp.sqrt(miss * miss + smoothing)
    crps = skill / members - spread_add / (2.0 * members * (members - 1))
    loss_part = jnp.sum(coef * crps)
    slope = miss / skill / members - pull_add / (1.0 * members * (members - 1))
    grad_x = (loss_scale * coef * slope).astype(jnp.bfloat16)
    grad_z = jnp.einsum("ov,vp->op", w_second, grad_x, preferred_element_type=jnp.float32)
    grad_pre = jax.vjp(jax.nn.gelu, pre)[1](grad_z)[0].astype(jnp.bfloat16)
    grad_feat = jnp.einsum(
        "io,op->ip", w_first, grad_pre, preferred_element_type=jnp.float32
    ).astype(jnp.bfloat16)
    part_w1 = jnp.einsum("ip,op->io", features, grad_pre, preferred_element_type=jnp.float32)
    part_w2 = jnp.einsum("op,vp->ov", hidden_act, grad_x, preferred_element_type=jnp.float32)
    part_b1 = jnp.sum(grad_pre.astype(jnp.float32), axis=1)
    part_b2 = jnp.sum(grad_x.astype(jnp.float32), axis=1)
    loss_sum, bias_sum = lax.psum((loss_part, part_b2), ("ens", "space"))
    whole_w1, whole_w2, whole_b1 = lax.psum((part_w1, part_w2, part_b1), ("ens", "space"))
    share = whole_w1.shape[0] // lax.axis_size("space")
    offset = lax.axis_index("space") * share
    sum_w1 = lax.dynamic_slice_in_dim(whole_w1, offset, share, 0)
    sum_w2 = lax.dynamic_slice_in_dim(whole_w2, offset, share, 0)
    sum_b1 = lax.dynamic_slice_in_dim(whole_b1, offset, share, 0)
    total_points = columns * lax.axis_size("space")
    factor = 1.0 / math.sqrt(members * total_points)
    loss = loss_sum / total_points
    return (
        loss,
        grad_feat[None],
        sum_w1 * factor,
        sum_b1 * factor,
        sum_w2 * factor,
        bias_sum * factor,
    )


def solution(mesh):
    in_specs = (P("ens", None, "space"), P(None, "space"), P("space"), P(), P(), P(), P(), P(), P())
    out_specs = (P(), P("ens", None, "space"), P("space", None), P("space"), P("space", None), P())
    return jax.shard_map(
        on_device, mesh=mesh, in_specs=in_specs, out_specs=out_specs, check_vma=False
    )
```

profile of v0, /device:TPU:97, one launch (start us, length us, event | category | flops | bytes accessed | tf_op | source)
XLA Modules:
  0.0 368.4 jit_solution(254239383439733305)
XLA Ops:
  7.2 0.0 copy-start
  7.2 0.0 copy-start.5
  7.2 0.0 copy-start.7
  7.2 0.0 copy-start.6
  7.2 0.0 copy-start.9
  7.2 0.0 all-gather.4.cloned.1.call-start
  7.3 1.5 copy-done
  8.8 7.0 %multiply_convert_fusion = (bf16[1024,1024]{0,1:T(8,128)(2,1)S(1)}, f32[1024,1024]{0,1:T(8,128)}) fusion(f32[1024]{0:T(1024)} %param.15, bf16[1024,1024]{1,0:T(8,128)(2,1)} %param.14, bf16[1,1024,1024]{2,1,0:T(8,128)(2,1)S(1)} %copy-done), kind=kOutput, calls=%fused_computation.15 | convolution fusion | flops 2157969408 | bytes 10489856 | tf_op jit(solution)/shard_map/io,ip->op/dot_general | solution.py:24
  15.7 0.0 copy-start.1
  15.7 1.3 copy-done.1
  17.1 0.0 copy-done.5
  17.1 0.0 copy-done.7
  17.1 0.0 copy-start.4
  17.1 0.0 copy-start.8
  17.1 1.6 convolution_add_fusion
  18.6 0.0 copy-start.3
  18.6 0.0 all-gather.4.cloned.1.call-update
  18.7 0.2 all-reduce.4.cloned.1.call-start
  18.9 0.0 copy-done.6
  18.9 0.0 copy-done.9
  18.9 1.5 fusion.13
  20.5 47.0 %all-gather.4.cloned.1.call-done = f32[8,100,1024]{2,1,0:T(8,128)} async-done(((f32[1,100,1024]{2,1,0:T(8,128)}), f32[8,100,1024]{2,1,0:T(8,128)}) %all-gather.4.cloned.1.call-update) | async-done | bytes 3276816 | tf_op jit(solution)/shard_map/all_gather | solution.py:39
  67.5 0.0 copy-start.2
  67.5 4.1 %fusion.12 = (f32[100,1024]{1,0:T(8,128)S(1)}, f32[100,1024]{1,0:T(8,128)S(1)}) fusion(f32[8,100,1024]{2,1,0:T(8,128)} %all-gather.4.cloned.1.call-done, f32[100,1024]{1,0:T(8,128)} %bitcast.45), kind=kLoop, calls=%fused_computation.19 | loop fusion | flops 4710400 | bytes 4505600 | tf_op jit(solution)/shard_map/reduce_sum | solution.py:14
  71.6 0.0 copy-start.10
  71.7 0.0 copy-start.12
  71.7 0.0 copy-done.4
  71.7 0.0 copy-done.8
  71.7 0.0 copy-done.3
  71.7 1.0 convert_reduce_fusion.1
  72.7 0.0 copy-done.2
  72.7 1.6 fusion.22
  74.3 0.0 copy-done.10
  74.3 0.0 copy-done.12
  74.3 3.5 convert_reduce_fusion
  77.8 0.0 copy-start.11
  77.8 1.3 copy-done.11
  79.1 4.4 %convolution_bitcast_fusion = f32[1024,1024]{0,1:T(8,128)} fusion(bf16[1024,1024]{0,1:T(8,128)(2,1)S(1)} %get-tuple-element.31, bf16[1,1024,1024]{2,1,0:T(8,128)(2,1)S(1)} %copy-done), kind=kOutput, calls=%fused_computation.22 | convolution fusion | flops 2147483648 | bytes 8388608 | tf_op jit(solution)/shard_map/ip,op->io/dot_general | solution.py:52
  83.5 0.0 all-reduce.4.cloned.1.call-update
  83.5 76.9 %all-reduce = (f32[]{:T(128)}, f32[1024]{0:T(1024)S(1)}, f32[100]{0:T(128)S(1)}) all-reduce(f32[]{:T(128)} %get-tuple-element.27, f32[1024]{0:T(1024)S(1)} %get-tuple-element.30, f32[100]{0:T(128)S(1)} %get-tuple-element.25), channel_id=1, replica_groups=mesh['ens'=8,'space'=32] {'ens','space'}, use_global_device_ids=true, to_apply=%region_2.0 | all-reduce | flops 1125 | bytes 9000 | tf_op jit(solution)/shard_map/psum | solution.py:56
  160.4 6.0 %convert_bitcast_fusion = bf16[1,1024,1024]{1,2,0:T(8,128)(2,1)} fusion(bf16[1024,1024]{0,1:T(8,128)(2,1)} %copy-done.11, bf16[1024,1024]{1,0:T(8,128)(2,1)} %param.14), kind=kOutput, calls=%fused_computation.26 | convolution fusion | flops 2148532224 | bytes 6291456 | tf_op jit(solution)/shard_map/io,op->ip/dot_general | solution.py:49
  166.3 3.9 %copy.17 = bf16[1,1024,1024]{2,1,0:T(8,128)(2,1)} copy(bf16[1,1024,1024]{1,2,0:T(8,128)(2,1)} %convert_bitcast_fusion) | data formatting | bytes 4194304
  170.9 0.6 dynamic-slice_multiply_fusion.2
  171.5 0.5 broadcast_multiply_fusion
  172.0 185.0 %all-reduce.4.cloned.1.call-done = (f32[1024,1024]{0,1:T(8,128)}, f32[1024,100]{1,0:T(8,128)}) async-done(((f32[1024,1024]{0,1:T(8,128)}, f32[1024,100]{1,0:T(8,128)}), (f32[1024,1024]{0,1:T(8,128)}, f32[1024,100]{1,0:T(8,128)})) %all-reduce.4.cloned.1.call-update) | async-done | bytes 4603920 | tf_op jit(solution)/shard_map/psum | solution.py:57
  357.0 1.2 dynamic-slice_multiply_fusion
  358.2 1.3 dynamic-slice_multiply_fusion.1
  359.6 0.8 copy.18
  (1 shorter events, 0.0 us)
Async XLA Ops:
  7.2 1.6 copy-start
  7.2 9.9 %copy-start.5 = (bf16[1024,100]{0,1:T(8,128)(2,1)S(1)}, bf16[1024,100]{0,1:T(8,128)(2,1)}, u32[]{:S(2)}) copy-start(bf16[1024,100]{0,1:T(8,128)(2,1)} %param.16) | copy-start | bytes 614404
  7.2 9.9 %copy-start.7 = (f32[100]{0:T(128)S(1)}, f32[100]{0:T(128)}, u32[]{:S(2)}) copy-start(f32[100]{0:T(128)} %param.17) | copy-start | bytes 1204
  7.2 11.7 %copy-start.6 = (f32[721]{0:T(1024)S(1)}, f32[721]{0:T(1024)}, u32[]{:S(2)}) copy-start(f32[721]{0:T(1024)} %param.12) | copy-start | bytes 8656
  7.2 11.7 %copy-start.9 = (s32[1024]{0:T(1024)S(1)}, s32[1024]{0:T(1024)}, u32[]{:S(2)}) copy-start(s32[1024]{0:T(1024)} %param.11) | copy-start | bytes 12292
  7.2 60.3 %all-gather.4.cloned.1.call-start = ((), (), s32[]{:S(2)}) async-start(), calls=%async_computation | async-start | bytes 3833856 | tf_op jit(solution)/shard_map/all_gather | solution.py:39
  15.7 1.3 copy-start.1
  17.1 54.6 %copy-start.4 = (f32[100,1024]{1,0:T(8,128)S(1)}, f32[100,1024]{1,0:T(8,128)}, u32[]{:S(2)}) copy-start(f32[100,1024]{1,0:T(8,128)} %param.10) | copy-start | bytes 1228804
  17.1 54.6 %copy-start.8 = (f32[100]{0:T(128)S(1)}, f32[100]{0:T(128)}, u32[]{:S(2)}) copy-start(f32[100]{0:T(128)} %param.13) | copy-start | bytes 1204
  18.6 53.0 %copy-start.3 = (f32[1024,100]{0,1:T(8,128)S(1)}, f32[1024,100]{0,1:T(8,128)}, u32[]{:S(2)}) copy-start(f32[1024,100]{0,1:T(8,128)} %convolution_add_fusion) | copy-start | bytes 1228804
  18.7 338.3 %all-reduce.4.cloned.1.call-start = ((), (), s32[]{:S(2)}) async-start(), calls=%async_computation.1 | async-start | bytes 9437184 | tf_op jit(solution)/shard_map/psum | solution.py:57
  67.5 5.2 %copy-start.2 = (bf16[1024,1024]{0,1:T(8,128)(2,1)S(1)}, bf16[1024,1024]{0,1:T(8,128)(2,1)}, u32[]{:S(2)}) copy-start(bf16[1024,1024]{0,1:T(8,128)(2,1)} %copy-done.1) | copy-start | bytes 6291460
  71.6 2.6 copy-start.10
  71.7 2.6 copy-start.12
  77.8 1.3 copy-start.11
Sparse Core Ops, SparseCore 0:
  18.8 48.6 all-gather.3
  83.6 273.3 all-reduce.3
where the time goes:
time: 369 us; the launch traced here: 368 us
  waiting for transfers between devices  232 us (63%)
  blocking collectives  76.9 us (21%)
  matrix products  25.5 us (7%)
  between operations  16 us (4%)
  local copies, waits for them, and re-layouts  8.95 us (2%)
  other arithmetic  8.84 us (2%)
    psum x1, waiting for transfers between devices, on_device(): lax.psum((part_w1, part_w2, part_b1), ('ens', 'space'))  185 us
    psum x1, blocking collectives, on_device(): loss_sum, bias_sum = lax.psum((loss_part, part_b2), ('ens', 'space'))  76.9 us
    all_gather x1, waiting for transfers between devices, on_device(): lax.all_gather(mine[None], 'ens', axis=0, tiled=True)  47 us
    unnamed x29, local copies, waits for them, and re-layouts  8.95 us
  transfers between devices with their start and end apart: 2, of which 2 were waited for; matrix products, arithmetic and copies ran while one was open for 3% of the time, Pallas kernels for 0%

commit v1 on v0

--- a/solution.py
+++ b/solution.py
@@ -54,7 +54,7 @@
     part_b1 = jnp.sum(grad_pre.astype(jnp.float32), axis=1)
     part_b2 = jnp.sum(grad_x.astype(jnp.float32), axis=1)
     loss_sum, bias_sum = lax.psum((loss_part, part_b2), ("ens", "space"))
-    whole_w1, whole_w2, whole_b1 = lax.psum((part_w1, part_w2, part_b1), ("ens", "space"))
+    whole_w1, whole_w2, whole_b1 = lax.psum(lax.psum((part_w1, part_w2, part_b1), "ens"), "space")
     share = whole_w1.shape[0] // lax.axis_size("space")
     offset = lax.axis_index("space") * share
     sum_w1 = lax.dynamic_slice_in_dim(whole_w1, offset, share, 0)

time: 369 us -> 522 us (1.41); the launches traced: 368 us -> 514 us
  blocking collectives: 76.9 us -> 160 us
  waiting for transfers between devices: 232 us -> 295 us
    psum x0 -> x2, blocking collectives: none -> 83.4 us  [the longest x1 69.6 us: on_device(): lax.psum(lax.psum((part_w1, part_w2, part_b1), 'ens'), 'space')]
    psum x1 -> x2, waiting for transfers between devices: 185 us -> 248 us  [the longest x1 127 us: on_device(): lax.psum(lax.psum((part_w1, part_w2, part_b1), 'ens'), 'space')]
  transfers between devices with their start and end apart: 2 -> 3, of which waited for: 2 -> 3; matrix products, arithmetic and copies ran while one was open for 3% -> 2% of each run, Pallas kernels for 0% -> 0%
where the time goes in v1:
time: 522 us; the launch traced here: 514 us
  waiting for transfers between devices  295 us (57%)
  blocking collectives  160 us (31%)
  matrix products  25.5 us (5%)
  between operations  15.7 us (3%)
  local copies, waits for them, and re-layouts  8.95 us (2%)
  other arithmetic  8.84 us (2%)
    psum x1, waiting for transfers between devices, on_device(): lax.psum(lax.psum((part_w1, part_w2, part_b1), 'ens'), 'space')  127 us
    psum x1, waiting for transfers between devices, on_device(): lax.psum((part_w1, part_w2, part_b1), 'ens')  120 us
    psum x1, blocking collectives, on_device(): loss_sum, bias_sum = lax.psum((loss_part, part_b2), ('ens', 'space'))  76.2 us
    psum x1, blocking collectives, on_device(): lax.psum(lax.psum((part_w1, part_w2, part_b1), 'ens'), 'space')  69.6 us
    all_gather x1, waiting for transfers between devices, on_device(): lax.all_gather(mine[None], 'ens', axis=0, tiled=True)  47 us
    psum x1, blocking collectives, on_device(): lax.psum((part_w1, part_w2, part_b1), 'ens')  13.8 us
  transfers between devices with their start and end apart: 3, of which 3 were waited for; matrix products, arithmetic and copies ran while one was open for 2% of the time, Pallas kernels for 0%

profile of v1, /device:TPU:97, one launch (start us, length us, event | category | flops | bytes accessed | tf_op | source)
XLA Modules:
  0.0 513.8 jit_solution(8124415390894110187)
XLA Ops:
  7.2 0.0 copy-start
  7.2 0.0 copy-start.5
  7.2 0.0 copy-start.7
  7.2 0.0 copy-start.6
  7.2 0.0 copy-start.9
  7.2 0.0 all-gather.4.cloned.1.call-start
  7.3 1.5 copy-done
  8.8 7.0 %multiply_convert_fusion = (bf16[1024,1024]{0,1:T(8,128)(2,1)S(1)}, f32[1024,1024]{0,1:T(8,128)}) fusion(f32[1024]{0:T(1024)} %param.15, bf16[1024,1024]{1,0:T(8,128)(2,1)} %param.14, bf16[1,1024,1024]{2,1,0:T(8,128)(2,1)S(1)} %copy-done), kind=kOutput, calls=%fused_computation.15 | convolution fusion | flops 2157969408 | bytes 10489856 | tf_op jit(solution)/shard_map/io,ip->op/dot_general | solution.py:24
  15.7 1.3 copy-done.1
  17.1 0.0 copy-done.5
  17.1 0.0 copy-done.7
  17.1 1.6 convolution_add_fusion
  18.6 0.0 all-gather.4.cloned.1.call-update
  18.7 0.2 all-reduce.8.cloned.1.call-start
  18.9 0.0 copy-done.6
  18.9 0.0 copy-done.9
  18.9 1.5 fusion.13
  20.5 47.0 %all-gather.4.cloned.1.call-done = f32[8,100,1024]{2,1,0:T(8,128)} async-done(((f32[1,100,1024]{2,1,0:T(8,128)}), f32[8,100,1024]{2,1,0:T(8,128)}) %all-gather.4.cloned.1.call-update) | async-done | bytes 3276816 | tf_op jit(solution)/shard_map/all_gather | solution.py:39
  67.5 4.1 fusion.12
  71.6 0.0 copy-start.10
  71.7 0.0 copy-start.12
  71.7 0.0 copy-done.4
  71.7 0.0 copy-done.8
  71.7 0.0 copy-done.3
  71.7 1.0 convert_reduce_fusion.1
  72.7 0.0 copy-done.2
  72.7 1.6 fusion.22
  74.3 0.0 copy-done.10
  74.3 0.0 copy-done.12
  74.3 3.5 convert_reduce_fusion
  77.8 0.0 copy-start.11
  77.8 1.3 copy-done.11
  79.1 4.4 convolution_bitcast_fusion
  83.5 0.0 all-reduce.8.cloned.1.call-update
  83.5 0.0 all-reduce.6.cloned.1.call-start
  83.6 120.4 %all-reduce.8.cloned.1.call-done = (f32[1024,1024]{0,1:T(8,128)}, f32[1024,100]{1,0:T(8,128)}) async-done(((f32[1024,1024]{0,1:T(8,128)}, f32[1024,100]{1,0:T(8,128)}), (f32[1024,1024]{0,1:T(8,128)}, f32[1024,100]{1,0:T(8,128)})) %all-reduce.8.cloned.1.call-update) | async-done | bytes 4603920 | tf_op jit(solution)/shard_map/psum | solution.py:57
  204.0 0.0 all-reduce.6.cloned.1.call-update
  204.0 76.2 %all-reduce = (f32[]{:T(128)}, f32[100]{0:T(128)S(1)}) all-reduce(f32[]{:T(128)} %get-tuple-element.28, f32[100]{0:T(128)S(1)} %get-tuple-element.26), channel_id=1, replica_groups=mesh['ens'=8,'space'=32] {'ens','space'}, use_global_device_ids=true, to_apply=%region_2.0 | all-reduce | flops 101 | bytes 808 | tf_op jit(solution)/shard_map/psum | solution.py:56
  280.2 6.0 %convert_bitcast_fusion = bf16[1,1024,1024]{1,2,0:T(8,128)(2,1)} fusion(bf16[1024,1024]{0,1:T(8,128)(2,1)} %copy-done.11, bf16[1024,1024]{1,0:T(8,128)(2,1)} %param.14), kind=kOutput, calls=%fused_computation.26 | convolution fusion | flops 2148532224 | bytes 6291456 | tf_op jit(solution)/shard_map/io,op->ip/dot_general | solution.py:49
  286.1 3.9 copy.17
  290.7 13.8 %psum.59 = f32[1024]{0:T(1024)S(1)} all-reduce(f32[1024]{0:T(1024)S(1)} %get-tuple-element.31), channel_id=1, replica_groups=mesh['ens'=8,'space'=32] {'ens'}, use_global_device_ids=true, to_apply=%region_7.0 | all-reduce | flops 1024 | bytes 8192 | tf_op jit(solution)/shard_map/psum | solution.py:57
  304.5 69.6 %psum.60 = f32[1024]{0:T(1024)S(1)} all-reduce(f32[1024]{0:T(1024)S(1)} %psum.59), channel_id=1, replica_groups=mesh['ens'=8,'space'=32] {'space'}, use_global_device_ids=true, to_apply=%region_8.0 | all-reduce | flops 1024 | bytes 8192 | tf_op jit(solution)/shard_map/psum | solution.py:57
  374.1 0.6 dynamic-slice_multiply_fusion.2
  374.7 0.5 broadcast_multiply_fusion
  375.2 127.5 %all-reduce.6.cloned.1.call-done = (f32[1024,1024]{0,1:T(8,128)}, f32[1024,100]{1,0:T(8,128)}) async-done(((f32[1024,1024]{0,1:T(8,128)}, f32[1024,100]{1,0:T(8,128)}), (f32[1024,1024]{0,1:T(8,128)}, f32[1024,100]{1,0:T(8,128)})) %all-reduce.6.cloned.1.call-update) | async-done | bytes 4603920 | tf_op jit(solution)/shard_map/psum | solution.py:57
  502.7 1.2 dynamic-slice_multiply_fusion
  504.0 1.3 dynamic-slice_multiply_fusion.1
  505.3 0.8 copy.18
  (6 shorter events, 0.0 us)
Async XLA Ops:
  7.2 1.6 copy-start
  7.2 9.9 %copy-start.5 = (bf16[1024,100]{0,1:T(8,128)(2,1)S(1)}, bf16[1024,100]{0,1:T(8,128)(2,1)}, u32[]{:S(2)}) copy-start(bf16[1024,100]{0,1:T(8,128)(2,1)} %param.16) | copy-start | bytes 614404
  7.2 9.9 %copy-start.7 = (f32[100]{0:T(128)S(1)}, f32[100]{0:T(128)}, u32[]{:S(2)}) copy-start(f32[100]{0:T(128)} %param.17) | copy-start | bytes 1204
  7.2 11.7 %copy-start.6 = (f32[721]{0:T(1024)S(1)}, f32[721]{0:T(1024)}, u32[]{:S(2)}) copy-start(f32[721]{0:T(1024)} %param.12) | copy-start | bytes 8656
  7.2 11.7 %copy-start.9 = (s32[1024]{0:T(1024)S(1)}, s32[1024]{0:T(1024)}, u32[]{:S(2)}) copy-start(s32[1024]{0:T(1024)} %param.11) | copy-start | bytes 12292
  7.2 60.3 %all-gather.4.cloned.1.call-start = ((), (), s32[]{:S(2)}) async-start(), calls=%async_computation | async-start | bytes 3833856 | tf_op jit(solution)/shard_map/all_gather | solution.py:39
  15.7 1.3 copy-start.1
  17.1 54.6 %copy-start.4 = (f32[100,1024]{1,0:T(8,128)S(1)}, f32[100,1024]{1,0:T(8,128)}, u32[]{:S(2)}) copy-start(f32[100,1024]{1,0:T(8,128)} %param.10) | copy-start | bytes 1228804
  17.1 54.6 %copy-start.8 = (f32[100]{0:T(128)S(1)}, f32[100]{0:T(128)}, u32[]{:S(2)}) copy-start(f32[100]{0:T(128)} %param.13) | copy-start | bytes 1204
  18.6 53.0 %copy-start.3 = (f32[1024,100]{0,1:T(8,128)S(1)}, f32[1024,100]{0,1:T(8,128)}, u32[]{:S(2)}) copy-start(f32[1024,100]{0,1:T(8,128)} %convolution_add_fusion) | copy-start | bytes 1228804
  18.7 185.3 %all-reduce.8.cloned.1.call-start = ((), (), s32[]{:S(2)}) async-start(), calls=%async_computation.2 | async-start | bytes 9437184 | tf_op jit(solution)/shard_map/psum | solution.py:57
  67.5 5.2 %copy-start.2 = (bf16[1024,1024]{0,1:T(8,128)(2,1)S(1)}, bf16[1024,1024]{0,1:T(8,128)(2,1)}, u32[]{:S(2)}) copy-start(bf16[1024,1024]{0,1:T(8,128)(2,1)} %copy-done.1) | copy-start | bytes 6291460
  71.6 2.7 copy-start.10
  71.7 2.7 copy-start.12
  77.8 1.3 copy-start.11
  83.5 419.2 %all-reduce.6.cloned.1.call-start = ((), (), s32[]{:S(2)}) async-start(), calls=%async_computation.1 | async-start | bytes 9437184 | tf_op jit(solution)/shard_map/psum | solution.py:57
Sparse Core Ops, SparseCore 0:
  18.8 48.6 all-gather.3
  83.6 120.2 all-reduce.7
  206.7 295.9 all-reduce.5
